TPU v7x, 32 devices: a whole 2x2x4 slice. The times are simulated.
32 devices in a mesh: group: 2 (over y), tp: 8 (over z, x), dp: 2 (over core).
Axes of the slice: x: 2, y: 2, z: 4, core: 2. Of those that a mesh axis runs over, the one named last changes fastest.
Arguments:
- hidden: bfloat16 [4, 384, 2, 8192], P(('group', 'dp'), None, None, 'tp'), parts along dimension 0, may hold values from -8 to 8
- norm_gain: bfloat16 [8192], replicated, may hold values from 0.5 to 1.5
- w_qkv: bfloat16 [8192, 64, 160], P(None, 'tp'), may hold values from -0.0625 to 0.0625
- adapter_store: bfloat16 [96, 8192, 128], P(('group', 'tp', 'dp')), parts along dimension 0, may hold values from -0.75 to 0.75
- adapter_home: int32 [96], P('group'), parts along dimension 0, may hold values from 0 to 47, as said below
- slot_adapter: int32 [4, 8], P('group'), parts along dimension 0, may hold values from 0 to 47, as said below
- request_slot: int32 [4, 384], P(('group', 'dp')), parts along dimension 0, may hold values from 0 to 7, as said below
- cache_kv: bfloat16 [4, 384, 128, 2048], P(('group', 'dp'), 'tp'), parts along dimension 0, may hold values from -240 to 240
- cache_len: int32 [4, 384], P(('group', 'dp'), 'tp'), parts along dimension 0, may hold values from 1 to 128
Outputs:
- attn_out: bfloat16 [4, 384, 2, 8192], P(('group', 'dp'), 'tp'), parts along dimension 0
- new_kv: bfloat16 [4, 384, 2, 2048], P(('group', 'dp'), 'tp'), parts along dimension 0
There are 2 independent parts, one for each index of `group`. A program takes and returns all parts, laid end to end along the dimension named above; an argument that names none is the same for every part. Nothing has to cross between parts.
Inputs may be any that keep to these rules, and one draw needn't show every extreme that they name: `adapter_home`: a permutation of the storage rows. Within one block, the numbers adapter_home[slot_adapter[n, s]] // 6 over its 8 slots are all different. `request_slot`: every slot of a block is used by some request of that block.
All inputs are finite; a program needn't handle non-finite values.
Results may differ from a plain program's by a relative error of at most 0.0031.
The roundings to bfloat16 on the way count: a program that leaves them out, or rounds other values in their place, can miss the bound.
Values may be sent and summed in bfloat16 or wider, within the bound.
A program may use at most 256 MiB of HBM per device.

v0:
```python
import jax
import jax.numpy as jnp
from jax import lax
from jax.sharding import PartitionSpec as P

D = 8192
HEADS = 64
KV_HEADS = 8
HEAD_WIDTH = 128
RANK = 64
CACHE = 128
ADAPT_DEV = 3
KEY_VALUE_SHARE = 32
GROUP = 8


adapter_scale = 0.0625
rope_base = 500000.0
norm_eps = 1e-05
masked_out = -1e30


def rotate(vectors, positions):
    halfway = vectors.shape[-1] // 2
    counter = jnp.arange(halfway, dtype=jnp.float32)
    inverse_freq = rope_base ** (-2.0 * counter / vectors.shape[-1])
    angles = positions[..., None] * inverse_freq
    cosine = jnp.cos(angles)
    sine_part = jnp.sin(angles)
    leading = vectors[..., :halfway]
    trailing = vectors[..., halfway:]
    return jnp.concatenate(
        [leading * cosine - trailing * sine_part, trailing * cosine + leading * sine_part], axis=-1
    )


def attend(query_rot, key_rot, value_new, cache_block, length_block):
    batch_count = query_rot.shape[0]
    grouped = query_rot.reshape(batch_count, 2, KV_HEADS, GROUP, HEAD_WIDTH)
    cache_keys = cache_block[:, :, : KV_HEADS * HEAD_WIDTH].reshape(
        batch_count, CACHE, KV_HEADS, HEAD_WIDTH
    )
    cache_values = cache_block[:, :, KV_HEADS * HEAD_WIDTH :].reshape(
        batch_count, CACHE, KV_HEADS, HEAD_WIDTH
    )
    factor = HEAD_WIDTH ** (-0.5)
    old_scores = (
        jnp.einsum("rpgjc,rlgc->rpgjl", grouped, cache_keys, preferred_element_type=jnp.float32)
        * factor
    )
    new_scores = (
        jnp.einsum("rpgjc,rngc->rpgjn", grouped, key_rot, preferred_element_type=jnp.float32)
        * factor
    )
    old_valid = jnp.arange(CACHE, dtype=jnp.int32)[None, :] < length_block[:, None]
    new_valid = jnp.arange(2, dtype=jnp.int32)[None, :] <= jnp.arange(2, dtype=jnp.int32)[:, None]
    old_scores = jnp.where(old_valid[:, None, None, None, :], old_scores, masked_out)
    new_scores = jnp.where(new_valid[None, :, None, None, :], new_scores, masked_out)
    highest = jnp.maximum(jnp.max(old_scores, axis=-1), jnp.max(new_scores, axis=-1))[..., None]
    old_exp = jnp.exp(old_scores - highest)
    new_exp = jnp.exp(new_scores - highest)
    denominator = jnp.sum(old_exp, axis=-1, keepdims=True) + jnp.sum(
        new_exp, axis=-1, keepdims=True
    )
    old_weights = (old_exp / denominator).astype(jnp.bfloat16)
    new_weights = (new_exp / denominator).astype(jnp.bfloat16)
    mixture = jnp.einsum(
        "rpgjl,rlgc->rpgjc", old_weights, cache_values, preferred_element_type=jnp.float32
    )
    mixture = mixture + jnp.einsum(
        "rpgjn,rngc->rpgjc", new_weights, value_new, preferred_element_type=jnp.float32
    )
    return mixture.astype(jnp.bfloat16).reshape(batch_count, 2, HEADS * HEAD_WIDTH)


def slot_delta(slot_slices, local_normed, chosen, count_of_rows, slot_count, local_width):
    down_matrix = jnp.transpose(slot_slices[:, :, :RANK], (1, 0, 2)).reshape(
        local_width, slot_count * RANK
    )
    partial_rank = jnp.dot(local_normed, down_matrix, preferred_element_type=jnp.float32).reshape(
        count_of_rows, slot_count, RANK
    )
    partial_rank = jnp.sum(jnp.where(chosen[:, :, None], partial_rank, 0.0), axis=1)
    lowrank = lax.psum(partial_rank, "tp").astype(jnp.bfloat16)
    spread = jnp.where(
        chosen[:, :, None], lowrank[:, None, :], jnp.zeros((), jnp.bfloat16)
    ).reshape(count_of_rows, slot_count * RANK)
    up_matrix = jnp.transpose(slot_slices[:, :, RANK:], (0, 2, 1)).reshape(
        slot_count * RANK, local_width
    )
    return jnp.dot(spread, up_matrix, preferred_element_type=jnp.float32)


def body(
    hidden,
    norm_gain,
    w_qkv,
    adapter_store,
    adapter_home,
    slot_adapter,
    request_slot,
    cache_kv,
    cache_len,
):
    tp_count = lax.axis_size("tp")
    dp_count = lax.axis_size("dp")
    tp_index = lax.axis_index("tp")
    dp_index = lax.axis_index("dp")
    requests = hidden.shape[1]
    local_width = hidden.shape[3]
    device_heads = w_qkv.shape[1]
    slot_count = slot_adapter.shape[1]
    count_of_rows = requests * 2
    flat_rows = hidden[0].reshape(count_of_rows, local_width)
    gain_wide = norm_gain.astype(jnp.float32)
    weights = w_qkv.reshape(D, device_heads * (HEAD_WIDTH + KEY_VALUE_SHARE))
    column_start = tp_index * local_width
    stored_rows = adapter_home[slot_adapter]
    block_rows = lax.dynamic_index_in_dim(stored_rows, dp_index, 0, keepdims=False)
    device_index = tp_index * dp_count + dp_index
    offsets = stored_rows - device_index * ADAPT_DEV
    local_slots = jnp.arange(ADAPT_DEV, dtype=jnp.int32)
    selector = jnp.any(offsets[:, :, None] == local_slots[None, None, :], axis=1).astype(
        jnp.bfloat16
    )
    row_slot = jnp.repeat(request_slot[0], 2)
    chosen = row_slot[:, None] == jnp.arange(slot_count, dtype=jnp.int32)[None, :]
    gathered = lax.all_gather(flat_rows, "tp", axis=1, tiled=True)
    widened = gathered.astype(jnp.float32)
    mean_square = jnp.mean(widened * widened, axis=1, keepdims=True)
    normed = (widened * lax.rsqrt(mean_square + norm_eps) * gain_wide).astype(jnp.bfloat16)
    local_normed = lax.dynamic_slice_in_dim(normed, column_start, local_width, 1)
    projected_whole = jnp.dot(normed, weights, preferred_element_type=jnp.float32)
    pieces = adapter_store.reshape(ADAPT_DEV, tp_count, local_width, 2 * RANK)
    outgoing = jnp.einsum(
        "bm,mtlk->tblk", selector, pieces, preferred_element_type=jnp.float32
    ).astype(jnp.bfloat16)
    outgoing = outgoing.reshape(tp_count * dp_count, local_width, 2 * RANK)
    incoming = lax.all_to_all(outgoing, ("tp", "dp"), split_axis=0, concat_axis=0, tiled=True)
    slot_slices = jnp.take(incoming, block_rows // ADAPT_DEV, axis=0)
    delta_query = slot_delta(
        slot_slices, local_normed, chosen, count_of_rows, slot_count, local_width
    )
    delta_padded_rows = jnp.pad(
        delta_query.reshape(count_of_rows, device_heads, HEAD_WIDTH),
        ((0, 0), (0, 0), (0, KEY_VALUE_SHARE)),
    )
    packed_columns = (
        projected_whole.reshape(count_of_rows, device_heads, HEAD_WIDTH + KEY_VALUE_SHARE)
        + adapter_scale * delta_padded_rows
    ).astype(jnp.bfloat16)
    packed_columns = packed_columns.reshape(requests, 2, device_heads, HEAD_WIDTH + KEY_VALUE_SHARE)
    arrived_heads = lax.all_to_all(packed_columns, "tp", split_axis=0, concat_axis=2, tiled=True)
    local_requests = arrived_heads.shape[0]
    query_part = arrived_heads[..., :HEAD_WIDTH]
    shared = arrived_heads[..., HEAD_WIDTH:].reshape(local_requests, 2, HEADS * KEY_VALUE_SHARE)
    key_new = shared[..., : KV_HEADS * HEAD_WIDTH].reshape(local_requests, 2, KV_HEADS, HEAD_WIDTH)
    value_new = shared[..., KV_HEADS * HEAD_WIDTH :].reshape(
        local_requests, 2, KV_HEADS, HEAD_WIDTH
    )
    lengths = cache_len[0]
    positions = (lengths[:, None] + jnp.arange(2, dtype=jnp.int32)[None, :]).astype(jnp.float32)
    query_rot = rotate(query_part.astype(jnp.float32), positions[..., None]).astype(jnp.bfloat16)
    key_rot = rotate(key_new.astype(jnp.float32), positions[..., None]).astype(jnp.bfloat16)
    attn_out = attend(query_rot, key_rot, value_new, cache_kv[0], lengths)
    new_kv = jnp.concatenate(
        [
            key_rot.reshape(local_requests, 2, KV_HEADS * HEAD_WIDTH),
            value_new.reshape(local_requests, 2, KV_HEADS * HEAD_WIDTH),
        ],
        axis=-1,
    )
    return (attn_out[None], new_kv[None])


def solution(mesh):
    placed = (
        P(("group", "dp"), None, None, "tp"),
        P(),
        P(None, "tp", None),
        P(("group", "tp", "dp"), None, None),
        P("group"),
        P("group", None),
        P(("group", "dp"), None),
        P(("group", "dp"), "tp", None, None),
        P(("group", "dp"), "tp"),
    )
    return jax.shard_map(
        body,
        mesh=mesh,
        in_specs=placed,
        out_specs=(P(("group", "dp"), "tp", None, None), P(("group", "dp"), "tp", None, None)),
        check_vma=False,
    )
```

profile of v0, /device:TPU:0, one launch (start us, length us, event | category | flops | bytes accessed | tf_op | source)
XLA Modules:
  0.0 476.1 jit_solution(937612518070503055)
XLA Ops:
  7.2 3.6 reshape_squeeze.3
  11.0 0.7 gather_fusion
  11.9 23.6 %fusion.11 = bf16[8,2,1024,128]{3,1,2,0:T(2,128)(2,1)S(1)} fusion(bf16[3,8,1024,128]{3,2,1,0:T(8,128)(2,1)} %bitcast.167, pred[2,3]{1,0:T(4,128)(4,1)S(1)} %fusion.55), kind=kOutput, calls=%fused_computation.13 | convolution fusion | flops 14680064 | bytes 10485766 | tf_op jit(solution)/shard_map/bm,mtlk->tblk/dot_general | solution.py:135
  35.6 2.8 copy.53
  38.4 7.8 %all-to-all-start = ((bf16[16,1024,128]{2,1,0:T(8,128)(2,1)}), bf16[16,1024,128]{2,1,0:T(8,128)(2,1)}, u32[]{:S(2)}, u32[]{:S(2)}) async-start(bf16[16,1024,128]{2,1,0:T(8,128)(2,1)} %bitcast.150), calls=%async_computation | async-start | bytes 8388608 | tf_op jit(solution)/shard_map/all_to_all | solution.py:139
  46.5 125.1 %all-to-all-done = bf16[16,1024,128]{2,1,0:T(8,128)(2,1)} async-done(((bf16[16,1024,128]{2,1,0:T(8,128)(2,1)}), bf16[16,1024,128]{2,1,0:T(8,128)(2,1)}, u32[]{:S(2)}, u32[]{:S(2)}) %all-to-all-start) | async-done | bytes 4194336 | tf_op jit(solution)/shard_map/all_to_all | solution.py:139
  171.6 3.1 gather_fusion.1
  174.8 0.3 broadcast_select_fusion
  175.1 2.1 slice_bitcast_fusion
  177.2 2.7 copy.54
  179.8 0.8 copy.55
  180.7 0.5 copy.56
  181.2 88.7 %all-gather.2.cloned.1.call-done = bf16[768,8192]{1,0:T(8,128)(2,1)} async-done(((bf16[768,1024]{1,0:T(8,128)(2,1)}), bf16[768,8192]{1,0:T(8,128)(2,1)}) %all-gather.2.cloned.1.call-update) | async-done | bytes 12582928 | tf_op jit(solution)/shard_map/all_gather | solution.py:128
  269.9 7.1 %fusion = f32[768]{0:T(1024)S(1)} fusion(bf16[768,8192]{1,0:T(8,128)(2,1)} %all-gather.2.cloned.1.call-done), kind=kLoop, calls=%fused_computation.4 | loop fusion | flops 18873600 | bytes 12585984 | tf_op jit(solution)/shard_map/reduce_sum | solution.py:130
  277.0 7.6 %fusion.2 = bf16[768,8192]{1,0:T(8,128)(2,1)S(1)} fusion(bf16[768,8192]{1,0:T(8,128)(2,1)} %all-gather.2.cloned.1.call-done, f32[8192]{0:T(1024)S(1)} %convert_element_type.59, f32[768]{0:T(1024)S(1)} %add_rsqrt_fusion), kind=kLoop, calls=%fused_computation.6 | loop fusion | flops 25165824 | bytes 25201664 | tf_op jit(solution)/shard_map/convert_element_type | solution.py:131
  284.6 4.5 copy-done.2
  289.1 1.0 select_reduce_fusion
  290.1 37.1 %all-reduce.2 = bf16[768,64]{0,1:T(8,128)(2,1)S(1)} all-reduce(f32[768,64]{0,1:T(8,128)S(1)} %select_reduce_fusion), channel_id=1, replica_groups=mesh['group'=2,'tp'=8,'dp'=2] {'tp'}, use_global_device_ids=true, to_apply=%region_3.4 | all-reduce | flops 49152 | bytes 294912 | tf_op jit(solution)/shard_map/psum | solution.py:84
  327.3 1.0 fusion.65
  328.3 20.9 %add_convert_fusion = bf16[768,8,160]{0,2,1:T(8,128)(2,1)S(1)} fusion(f32[768,8,128]{0,2,1:T(8,128)S(1)} %fusion.65, bf16[8192,8,160]{0,2,1:T(8,128)(2,1)} %param.11, bf16[768,8192]{1,0:T(8,128)(2,1)} %copy-done.2), kind=kOutput, calls=%fused_computation.14 | convolution fusion | flops 16109076480 | bytes 38666240 | tf_op jit(solution)/shard_map/dot_general | solution.py:133
  349.2 3.5 copy.58
  352.8 3.6 all-to-all-start.1
  356.4 32.7 %copy.62 = bf16[1,48,128,2048]{2,3,1,0:T(8,128)(2,1)} copy(bf16[1,48,128,2048]{3,2,1,0:T(8,128)(2,1)} %param.16) | data formatting | bytes 50331648 | tf_op args[7]
  389.3 1.4 multiply_cosine_fusion
  390.7 17.3 %fusion.61 = (bf16[48,128,1024]{1,2,0:T(8,128)(2,1)}, bf16[48,128,1024]{1,2,0:T(8,128)(2,1)}) fusion(bf16[48,128,2048]{1,2,0:T(8,128)(2,1)} %bitcast.148), kind=kLoop, calls=%fused_computation.91 | loop fusion | bytes 50331648 | tf_op jit(solution)/shard_map/slice | solution.py:43
  408.0 13.2 %all-to-all-done.1 = bf16[384,2,8,160]{3,2,1,0:T(8,128)(2,1)S(1)} async-done(((bf16[384,2,8,160]{3,2,1,0:T(8,128)(2,1)}), bf16[384,2,8,160]{3,2,1,0:T(8,128)(2,1)S(1)}, u32[]{:S(2)}, u32[]{:S(2)}) %all-to-all-start.1) | async-done | bytes 1966112 | tf_op jit(solution)/shard_map/all_to_all | solution.py:153
  421.2 0.4 copy.124
  421.6 1.5 slice.58
  423.1 0.4 slice_convert_fusion
  423.5 3.2 reshape.298
  426.7 0.3 fusion.62
  427.3 0.2 copy-done.7
  427.5 1.3 fusion.21
  428.8 0.8 multiply_subtract_fusion
  429.6 0.5 maximum_convert_fusion
  430.2 0.7 copy.70
  430.9 7.9 %fusion.64 = (f32[48,2,8,8]{3,1,2,0:T(2,128)S(1)}, f32[48,2,8,8,2]{3,4,1,2,0:T(2,128)S(1)}) fusion(bf16[48,2,8,128]{3,1,2,0:T(2,128)(2,1)S(1)} %maximum_convert_fusion, pred[2,2]{1,0:T(4,128)(4,1)S(1)} %iota_compare_fusion.3, bf16[48,2,8,8,64]{4,3,2,1,0:T(8,128)(2,1)S(1)} %get-tuple-element.14, bf16[48,2,8,8,64]{4,3,2,1,0:T(8,128)(2,1)S(1)} %get-tuple-element.13), kind=kOutput, calls=%fused_computation.94 | convolution fusion | flops 6322176 | bytes 1843204 | tf_op jit(solution)/shard_map/rpgjc,rngc->rpgjn/dot_general | solution.py:52
  438.8 8.2 %bitcast_reduce_fusion = (f32[48,2,8,8]{3,1,2,0:T(2,128)S(1)}, f32[48,8,2,8,128]{4,3,2,1,0:T(8,128)S(1)}) fusion(pred[48,128]{1,0:T(8,128)(4,1)S(1)} %iota_compare_fusion.1, bf16[48,128,8,128,1]{1,3,4,2,0:T(8,128)(2,1)} %bitcast.149, bf16[48,2,8,8,64]{4,3,2,1,0:T(8,128)(2,1)S(1)} %get-tuple-element.14, bf16[48,2,8,8,64]{4,3,2,1,0:T(8,128)(2,1)S(1)} %get-tuple-element.13), kind=kOutput, calls=%fused_computation.18 | convolution fusion | flops 206825472 | bytes 17332224 | tf_op jit(solution)/shard_map/rpgjc,rlgc->rpgjl/dot_general | solution.py:48
  447.0 0.2 max.7
  447.2 2.3 fusion.16
  449.5 1.5 fusion.49
  451.1 0.7 copy-done.3
  451.9 0.2 add.104
  452.1 2.8 fusion.50
  454.9 9.2 %fusion.14 = bf16[48,2,8,8,128]{4,3,1,2,0:T(8,128)(2,1)} fusion(f32[48,8,128,2,8]{2,4,3,1,0:T(8,128)} %fusion.50, bf16[48,128,8,128,1]{1,3,4,2,0:T(8,128)(2,1)S(1)} %bitcast.157, f32[48,8,2,8,128]{4,3,2,1,0:T(8,128)S(1)} %get-tuple-element.26, f32[48,2,8,8]{3,1,2,0:T(2,128)} %copy-done.9, f32[48,2,8,8]{3,1,2,0:T(2,128)S(1)} %max.7, ...), kind=kOutput, calls=%fused_computation.16 | convolution fusion | flops 206831616 | bytes 20502528 | tf_op jit(solution)/shard_map/rpgjl,rlgc->rpgjc/dot_general | solution.py:67
  464.0 1.8 copy.88
  465.9 1.8 reshape.299
  467.9 1.2 copy.72
  (61 shorter events, 1.5 us)
Async XLA Ops:
  7.2 3.9 copy-start
  7.2 3.7 copy-start.13
  7.2 262.7 %all-gather.2.cloned.1.call-start = ((), (), s32[]{:S(2)}) async-start(), calls=%async_computation.2 | async-start | bytes 14155776 | tf_op jit(solution)/shard_map/all_gather | solution.py:128
  38.4 7.8 %copy-start.12 = (s32[1,384]{1,0:T(1,128)S(1)}, s32[1,384]{1,0:T(1,128)}, u32[]{:S(2)}) copy-start(s32[1,384]{1,0:T(1,128)} %param.15) | copy-start | bytes 4612
  38.4 8.1 %copy-start.10 = (bf16[8192]{0:T(1024)(128)(2,1)S(1)}, bf16[8192]{0:T(1024)(128)(2,1)}, u32[]{:S(2)}) copy-start(bf16[8192]{0:T(1024)(128)(2,1)} %param.10) | copy-start | bytes 49156
  38.4 133.3 %all-to-all-start = ((bf16[16,1024,128]{2,1,0:T(8,128)(2,1)}), bf16[16,1024,128]{2,1,0:T(8,128)(2,1)}, u32[]{:S(2)}, u32[]{:S(2)}) async-start(bf16[16,1024,128]{2,1,0:T(8,128)(2,1)} %bitcast.150), calls=%async_computation | async-start | bytes 8388608 | tf_op jit(solution)/shard_map/all_to_all | solution.py:139
  277.0 12.1 %copy-start.5 = (bf16[1024,8,64]{0,2,1:T(8,128)(2,1)S(1)}, bf16[1024,8,64]{0,2,1:T(8,128)(2,1)}, u32[]{:S(2)}) copy-start(bf16[1024,8,64]{0,2,1:T(8,128)(2,1)} %copy.54) | copy-start | bytes 3145732
  284.6 4.5 copy-start.2
  352.8 68.4 %all-to-all-start.1 = ((bf16[384,2,8,160]{3,2,1,0:T(8,128)(2,1)}), bf16[384,2,8,160]{3,2,1,0:T(8,128)(2,1)S(1)}, u32[]{:S(2)}, u32[]{:S(2)}) async-start(bf16[384,2,8,160]{3,2,1,0:T(8,128)(2,1)} %bitcast.152), calls=%async_computation.1 | async-start | bytes 6291456 | tf_op jit(solution)/shard_map/all_to_all | solution.py:153
  356.4 32.7 %copy-start.11 = (s32[1,48]{1,0:T(1,128)S(1)}, s32[1,48]{1,0:T(1,128)}, u32[]{:S(2)}) copy-start(s32[1,48]{1,0:T(1,128)} %param.17) | copy-start | bytes 580
  426.7 0.8 copy-start.7
  426.7 0.8 copy-start.8
  438.7 16.1 %slice-start = ((s8[12582912]{0:T(1024)(128)(4,1)}), s8[4194304]{0:T(1024)(128)(4,1)S(1)}, s32[]{:S(2)}) async-start(s8[12582912]{0:T(1024)(128)(4,1)} %bitcast.155), calls=%async_computation.3 | async-start | bytes 8388608
  438.7 16.1 %slice-start.1 = ((s8[12582912]{0:T(1024)(128)(4,1)}), s8[4194304]{0:T(1024)(128)(4,1)S(1)}, s32[]{:S(2)}) async-start(s8[12582912]{0:T(1024)(128)(4,1)} %bitcast.155), calls=%async_computation.4 | async-start | bytes 8388608
  451.1 0.7 copy-start.3
  451.8 3.0 slice-start.2
  452.1 2.8 copy-start.9
  464.0 3.7 copy-start.6
  464.0 3.8 copy-start.4
  464.0 5.0 %copy-start.1 = (s32[48]{0:T(128)S(1)}, s32[48]{0:T(128)}, u32[]{:S(2)}) copy-start(s32[48]{0:T(128)} %param.13) | copy-start | bytes 580
Sparse Core Ops, SparseCore 0:
  11.0 258.8 all-gather.1
where the time goes:
time: 484 us; the launch traced here: 476 us
  waiting for transfers between devices  227 us (47%)
  local copies, waits for them, and re-layouts  87.1 us (18%)
  matrix products  74.6 us (15%)
  blocking collectives  37.1 us (8%)
  other arithmetic  24.1 us (5%)
  between operations  14.7 us (3%)
  starting transfers between devices  11.5 us (2%)
    all_to_all x1, waiting for transfers between devices, body(): lax.all_to_all(outgoing, ('tp', 'dp'), split_axis=0, concat_axis=0, tiled...  125 us
    all_gather x1, waiting for transfers between devices, body(): gathered = lax.all_gather(flat_rows, 'tp', axis=1, tiled=True)  88.7 us
    unnamed x41, local copies, waits for them, and re-layouts  43.1 us
    psum x1, blocking collectives, slot_delta(): lowrank = lax.psum(partial_rank, 'tp').astype(jnp.bfloat16)  37.1 us
    dot_general x1, matrix products, body(): jnp.einsum('bm,mtlk->tblk', selector, pieces, preferred_element_type=jnp....  23.6 us
    dot_general x1, matrix products, body(): jnp.dot(normed, weights, preferred_element_type=jnp.float32)  20.9 us
    slice x1, local copies, waits for them, and re-layouts, attend(): cache_block[:, :, KV_HEADS * HEAD_WIDTH:]  17.3 us
    all_to_all x1, waiting for transfers between devices, body(): lax.all_to_all(packed_columns, 'tp', split_axis=0, concat_axis=2, tiled=T...  13.2 us
  transfers between devices with their start and end apart: 3, of which 3 were waited for; matrix products, arithmetic and copies ran while one was open for 19% of the time, Pallas kernels for 0%

commit v1 on v0

--- a/solution.py
+++ b/solution.py
@@ -1,6 +1,10 @@
+import functools
+
 import jax
 import jax.numpy as jnp
 from jax import lax
+from jax.experimental import pallas as pl
+from jax.experimental.pallas import tpu as pltpu
 from jax.sharding import PartitionSpec as P
 
 D = 8192
@@ -91,7 +95,7 @@
     return jnp.dot(spread, up_matrix, preferred_element_type=jnp.float32)
 
 
-def body(
+def plain_body(
     hidden,
     norm_gain,
     w_qkv,
@@ -173,6 +177,545 @@
     return (attn_out[None], new_kv[None])
 
 
+SPLIT = 2
+COLUMN_TILE = 256
+MESH_ID = pl.DeviceIdType.MESH
+
+
+def ring_to_tp(place, n):
+    high = place // (n // 2)
+    return (1 - high) * (2 * place) + high * (2 * (n - 1 - place) + 1)
+
+
+def project_kernel(
+    n,
+    hidden_ref,
+    gain_ref,
+    weight_ref,
+    up_ref,
+    chip_ref,
+    query_out,
+    shared_out,
+    normed,
+    weight_buf,
+    total,
+    query_send,
+    shared_send,
+    up_all,
+    sums_send,
+    sums_all,
+    reduce_send,
+    reduce_recv,
+    lowrank_all,
+    weight_sem,
+    ring_send,
+    ring_recv,
+    sums_send_sem,
+    sums_recv_sem,
+    up_send_sem,
+    up_recv_sem,
+    reduce_send_sem,
+    reduce_recv_sem,
+    spread_send_sem,
+    spread_recv_sem,
+    shared_send_sem,
+    shared_recv_sem,
+    query_send_sem,
+    query_recv_sem,
+):
+    me = lax.axis_index("tp")
+    rows, width = hidden_ref.shape
+    own_rows = rows // n
+    query_width = query_send.shape[1]
+    shared_width = shared_send.shape[1]
+    piece = rows // 2 // SPLIT
+
+    def peer(d):
+        return lax.rem(me + d, n)
+
+    def source(d):
+        return lax.rem(me + n - d, n)
+
+    def rows_of(t):
+        return pl.ds(pl.multiple_of(t * own_rows, own_rows), own_rows)
+
+    def remote(src, dst, send_sem, recv_sem, target):
+        return pltpu.make_async_remote_copy(
+            src_ref=src,
+            dst_ref=dst,
+            send_sem=send_sem,
+            recv_sem=recv_sem,
+            device_id={"tp": target},
+            device_id_type=MESH_ID,
+        )
+
+    barrier = pltpu.get_barrier_semaphore()
+    for d in range(1, n):
+        pl.semaphore_signal(barrier, inc=1, device_id={"tp": peer(d)}, device_id_type=MESH_ID)
+
+    def weight_copy(block):
+        return pltpu.make_async_copy(
+            weight_ref.at[block], weight_buf.at[block], weight_sem.at[block]
+        )
+
+    for block in range(n):
+        weight_copy(block).start()
+
+    sums_send[...] = jnp.zeros_like(sums_send)
+    for i in range(rows // 128):
+        wide = hidden_ref[i * 128 : (i + 1) * 128, :].astype(jnp.float32)
+        square = jnp.sum(wide * wide, axis=1, keepdims=True)
+        sums_send[i : i + 1, :] = jnp.transpose(jnp.broadcast_to(square, (128, 128)))[0:1, :]
+    sums_all[me] = sums_send[...]
+    pl.semaphore_wait(barrier, n - 1)
+
+    def sums_copy(d):
+        return remote(
+            sums_send, sums_all.at[me], sums_send_sem.at[d], sums_recv_sem.at[d], peer(d)
+        )
+
+    for d in range(1, n):
+        sums_copy(d).start()
+    for d in range(1, n):
+        sums_copy(d).wait_recv()
+    sums = sums_all[0]
+    for t in range(1, n):
+        sums = sums + sums_all[t]
+    scale = lax.rsqrt(sums / (n * width) + norm_eps)
+    for i in range(rows // 128):
+        span = slice(i * 128, (i + 1) * 128)
+        column = jnp.transpose(jnp.broadcast_to(scale[i : i + 1, :], (128, 128)))[:, 0:1]
+        wide = hidden_ref[span, :].astype(jnp.float32)
+        normed[me, span, :] = (wide * column * gain_ref[...]).astype(jnp.bfloat16)
+
+    odd = lax.rem(me, 2)
+    place = (1 - odd) * (me // 2) + odd * ((2 * n - 1 - me) // 2)
+    right = ring_to_tp(lax.rem(place + 1, n), n)
+    left = ring_to_tp(lax.rem(place + n - 1, n), n)
+
+    def ring_part(direction, i):
+        step, part = i // SPLIT, i % SPLIT
+        if direction == 0:
+            owner = ring_to_tp(lax.rem(place + n - step, n), n)
+        else:
+            owner = ring_to_tp(lax.rem(place + step, n), n)
+        start = direction * (rows // 2) + part * piece
+        if not isinstance(start, int):
+            start = pl.multiple_of(start, piece)
+        return owner, pl.ds(start, piece)
+
+    def ring_copy(direction, i):
+        owner, span = ring_part(direction, i)
+        block = normed.at[owner, span]
+        return remote(
+            block,
+            block,
+            ring_send.at[direction, i],
+            ring_recv.at[direction, i],
+            left if direction else right,
+        )
+
+    def compute(i):
+        parts = [ring_part(direction, i) for direction in range(2)]
+
+        @pl.loop(0, total.shape[1] // COLUMN_TILE)
+        def _(j):
+            columns = pl.ds(pl.multiple_of(j * COLUMN_TILE, COLUMN_TILE), COLUMN_TILE)
+            for owner, span in parts:
+                total[span, columns] += jnp.dot(
+                    normed[owner, span, :],
+                    weight_buf[owner, :, columns],
+                    preferred_element_type=jnp.float32,
+                )
+
+    for i in range(SPLIT):
+        for direction in range(2):
+            ring_copy(direction, i).start()
+
+    def up_copy(d):
+        return remote(
+            up_ref.at[peer(d)], up_all.at[me], up_send_sem.at[d], up_recv_sem.at[d], peer(d)
+        )
+
+    for d in range(1, n):
+        up_copy(d).start()
+    up_all[me] = up_ref[me]
+    total[...] = jnp.zeros_like(total)
+    for block in range(n):
+        weight_copy(block).wait()
+
+    def first(i, _):
+        compute(i)
+        return 0
+
+    lax.fori_loop(0, SPLIT, first, 0)
+
+    def middle(i, _):
+        for direction in range(2):
+            ring_copy(direction, i - SPLIT).wait_recv()
+            ring_copy(direction, i).start()
+        compute(i)
+        return 0
+
+    lax.fori_loop(SPLIT, (n - 1) * SPLIT, middle, 0)
+
+    def last(i, _):
+        for direction in range(2):
+            ring_copy(direction, i - SPLIT).wait_recv()
+        compute(i)
+        return 0
+
+    lax.fori_loop((n - 1) * SPLIT, n * SPLIT, last, 0)
+
+    low_column = query_width + shared_width
+    for t in range(n):
+        span = slice(t * own_rows, (t + 1) * own_rows)
+        low = total[span, low_column : low_column + 128]
+        reduce_send[span, :] = jnp.where(chip_ref[span, :] == me, low, 0.0).astype(jnp.bfloat16)
+
+    def reduce_copy(d):
+        return remote(
+            reduce_send.at[rows_of(peer(d))],
+            reduce_recv.at[me],
+            reduce_send_sem.at[d],
+            reduce_recv_sem.at[d],
+            peer(d),
+        )
+
+    for d in range(1, n):
+        reduce_copy(d).start()
+    reduce_recv[me] = reduce_send[rows_of(me), :]
+
+    shared_send[...] = total[:, query_width:low_column].astype(jnp.bfloat16)
+
+    def shared_copy(d):
+        return remote(
+            shared_send.at[rows_of(peer(d))],
+            shared_out.at[me],
+            shared_send_sem.at[d],
+            shared_recv_sem.at[d],
+            peer(d),
+        )
+
+    for d in range(1, n):
+        reduce_copy(d).wait_recv()
+    low = reduce_recv[0].astype(jnp.float32)
+    for t in range(1, n):
+        low = low + reduce_recv[t].astype(jnp.float32)
+    lowrank_all[me] = low.astype(jnp.bfloat16)
+
+    def spread_copy(d):
+        return remote(
+            lowrank_all.at[me],
+            lowrank_all.at[me],
+            spread_send_sem.at[d],
+            spread_recv_sem.at[d],
+            peer(d),
+        )
+
+    for d in range(1, n):
+        spread_copy(d).start()
+    for d in range(1, n):
+        shared_copy(d).start()
+    shared_out[me] = shared_send[rows_of(me), :]
+    for d in range(1, n):
+        up_copy(d).wait_recv()
+    for d in range(1, n):
+        spread_copy(d).wait_recv()
+
+    def mixed(t):
+        low = lowrank_all[t].astype(jnp.float32)
+        chip = chip_ref[rows_of(t), :]
+        tiles = []
+        for pair in range(n // 2):
+            even_part = jnp.where(chip == 2 * pair, low, 0.0)
+            odd_part = jnp.where(chip == 2 * pair + 1, low, 0.0)
+            tiles.append((even_part + pltpu.roll(odd_part, RANK, 1)).astype(jnp.bfloat16))
+        spread = jnp.concatenate(tiles, axis=1)
+        up = up_all[...].reshape(n * RANK, query_width)
+        delta = jnp.dot(spread, up, preferred_element_type=jnp.float32)
+        query = total[rows_of(t), 0:query_width]
+        return (query + adapter_scale * delta).astype(jnp.bfloat16)
+
+    def query_copy(d):
+        return remote(
+            query_send.at[rows_of(peer(d))],
+            query_out.at[me],
+            query_send_sem.at[d],
+            query_recv_sem.at[d],
+            peer(d),
+        )
+
+    def send_query(d, _):
+        query_send[rows_of(peer(d)), :] = mixed(peer(d))
+        query_copy(d).start()
+        return 0
+
+    lax.fori_loop(1, n, send_query, 0)
+    query_out[me] = mixed(me)
+
+    for d in range(1, n):
+        shared_copy(d).wait_recv()
+        query_copy(d).wait_recv()
+
+    def drain(i, _):
+        for direction in range(2):
+            ring_copy(direction, i).wait_send()
+        return 0
+
+    lax.fori_loop(0, (n - 1) * SPLIT, drain, 0)
+    for d in range(1, n):
+        sums_copy(d).wait_send()
+        up_copy(d).wait_send()
+        reduce_copy(d).wait_send()
+        spread_copy(d).wait_send()
+        shared_copy(d).wait_send()
+        query_copy(d).wait_send()
+
+
+def project_rows(n, hidden, gain, weight, up, chip):
+    rows, width = hidden.shape
+    columns = weight.shape[2]
+    own_rows = rows // n
+    query_width = up.shape[2]
+    shared_width = query_width // HEAD_WIDTH * KEY_VALUE_SHARE
+    dma = pltpu.SemaphoreType.DMA
+    vmem = pl.BlockSpec(memory_space=pltpu.VMEM)
+    bf16, f32 = jnp.bfloat16, jnp.float32
+    return pl.pallas_call(
+        functools.partial(project_kernel, n),
+        out_shape=(
+            jax.ShapeDtypeStruct((n, own_rows, query_width), bf16),
+            jax.ShapeDtypeStruct((n, own_rows, shared_width), bf16),
+        ),
+        in_specs=[vmem, vmem, pl.BlockSpec(memory_space=pl.ANY), vmem, vmem],
+        out_specs=(vmem, vmem),
+        scratch_shapes=[
+            pltpu.VMEM((n, rows, width), bf16),
+            pltpu.VMEM((n, width, columns), bf16),
+            pltpu.VMEM((rows, columns), f32),
+            pltpu.VMEM((rows, query_width), bf16),
+            pltpu.VMEM((rows, shared_width), bf16),
+            pltpu.VMEM((n, RANK, query_width), bf16),
+            pltpu.VMEM((8, 128), f32),
+            pltpu.VMEM((n, 8, 128), f32),
+            pltpu.VMEM((rows, 128), bf16),
+            pltpu.VMEM((n, own_rows, 128), bf16),
+            pltpu.VMEM((n, own_rows, 128), bf16),
+            dma((n,)),
+            dma((2, (n - 1) * SPLIT)),
+            dma((2, (n - 1) * SPLIT)),
+        ]
+        + [dma((n,))] * 12,
+        compiler_params=pltpu.CompilerParams(
+            collective_id=0, has_side_effects=True, vmem_limit_bytes=60 * 1024 * 1024
+        ),
+        cost_estimate=pl.CostEstimate(
+            flops=2 * rows * width * n * columns,
+            bytes_accessed=2 * n * width * columns,
+            transcendentals=0,
+        ),
+    )(hidden, gain, weight, up, chip)
+
+
+def attend_kernel(
+    length_ref, query_ref, cos_ref, sin_ref, new_ref, cache_ref, out_ref
+):
+    count = query_ref.shape[0]
+    lanes = KV_HEADS * HEAD_WIDTH
+    pad = new_ref.shape[1]
+    first = pl.program_id(0) * count
+    factor = HEAD_WIDTH ** (-0.5)
+    row = lax.broadcasted_iota(jnp.int32, (2 * HEADS, lanes), 0)
+    lane = lax.broadcasted_iota(jnp.int32, (2 * HEADS, lanes), 1)
+    own = (row // GROUP) % KV_HEADS == lane // HEAD_WIDTH
+    key_at = lax.broadcasted_iota(jnp.int32, (2 * HEADS, CACHE), 1)
+    new_at = lax.broadcasted_iota(jnp.int32, (2 * HEADS, pad), 1)
+    new_limit = lax.broadcasted_iota(jnp.int32, (2 * HEADS, pad), 0) // HEADS
+    across = (((1,), (1,)), ((), ()))
+    for b in range(count):
+        query = query_ref[b].astype(jnp.float32)
+        turned = pltpu.roll(query, HEAD_WIDTH // 2, 1)
+        rotated = jnp.concatenate(
+            [
+                query[p * HEADS : (p + 1) * HEADS] * cos_ref[b, p : p + 1, :]
+                + turned[p * HEADS : (p + 1) * HEADS] * sin_ref[b, p : p + 1, :]
+                for p in range(2)
+            ],
+            axis=0,
+        ).astype(jnp.bfloat16)
+        wide = jnp.concatenate([rotated] * KV_HEADS, axis=1)
+        wide = jnp.where(own, wide, jnp.zeros((), jnp.bfloat16))
+        old = (
+            lax.dot_general(
+                wide, cache_ref[b, :, 0:lanes], across, preferred_element_type=jnp.float32
+            )
+            * factor
+        )
+        new = (
+            lax.dot_general(
+                wide, new_ref[b, :, 0:lanes], across, preferred_element_type=jnp.float32
+            )
+            * factor
+        )
+        old = jnp.where(key_at < length_ref[first + b], old, masked_out)
+        new = jnp.where(new_at <= new_limit, new, masked_out)
+        highest = jnp.maximum(
+            jnp.max(old, axis=1, keepdims=True), jnp.max(new, axis=1, keepdims=True)
+        )
+        old_exp = jnp.exp(old - highest)
+        new_exp = jnp.exp(new - highest)
+        denominator = jnp.sum(old_exp, axis=1, keepdims=True) + jnp.sum(
+            new_exp, axis=1, keepdims=True
+        )
+        old_weights = (old_exp / denominator).astype(jnp.bfloat16)
+        new_weights = (new_exp / denominator).astype(jnp.bfloat16)
+        mixture = jnp.dot(
+            old_weights, cache_ref[b, :, lanes:], preferred_element_type=jnp.float32
+        ) + jnp.dot(new_weights, new_ref[b, :, lanes:], preferred_element_type=jnp.float32)
+        pieces = []
+        for p in range(2):
+            for g in range(KV_HEADS):
+                start = p * HEADS + g * GROUP
+                pieces.append(
+                    mixture[start : start + GROUP, g * HEAD_WIDTH : (g + 1) * HEAD_WIDTH]
+                )
+        out_ref[b] = jnp.concatenate(pieces, axis=0).astype(jnp.bfloat16)
+
+
+def attend_rows(lengths, query, cosine, sine, new, cache):
+    requests = query.shape[0]
+    block = 4
+
+    def spec(*shape):
+        return pl.BlockSpec((block,) + shape, lambda i: (i,) + (0,) * len(shape))
+
+    return pl.pallas_call(
+        attend_kernel,
+        grid=(requests // block,),
+        out_shape=jax.ShapeDtypeStruct((requests, 2 * HEADS, HEAD_WIDTH), jnp.bfloat16),
+        in_specs=[
+            pl.BlockSpec(memory_space=pltpu.SMEM),
+            spec(2 * HEADS, HEAD_WIDTH),
+            spec(2, HEAD_WIDTH),
+            spec(2, HEAD_WIDTH),
+            spec(new.shape[1], new.shape[2]),
+            spec(CACHE, cache.shape[2]),
+        ],
+        out_specs=spec(2 * HEADS, HEAD_WIDTH),
+        compiler_params=pltpu.CompilerParams(vmem_limit_bytes=32 * 1024 * 1024),
+        cost_estimate=pl.CostEstimate(
+            flops=4 * requests * 2 * HEADS * HEAD_WIDTH * CACHE * KV_HEADS,
+            bytes_accessed=2 * requests * CACHE * cache.shape[2],
+            transcendentals=requests * 2 * HEADS * CACHE,
+        ),
+    )(lengths, query, cosine, sine, new, cache)
+
+
+def ring_body(
+    tp_count,
+    dp_count,
+    hidden,
+    norm_gain,
+    w_qkv,
+    adapter_store,
+    adapter_home,
+    slot_adapter,
+    request_slot,
+    cache_kv,
+    cache_len,
+):
+    tp_index = lax.axis_index("tp")
+    dp_index = lax.axis_index("dp")
+    requests = hidden.shape[1]
+    local_width = hidden.shape[3]
+    device_heads = w_qkv.shape[1]
+    local_requests = requests // tp_count
+    rows = requests * 2
+    column_start = tp_index * local_width
+
+    per_chip = dp_count * ADAPT_DEV
+    stored_rows = adapter_home[slot_adapter]
+    slot_chip = stored_rows // per_chip
+    within = jnp.sum(jnp.where(slot_chip == tp_index, stored_rows % per_chip, 0), axis=1)
+    holder, local_slot = within // ADAPT_DEV, within % ADAPT_DEV
+    other = 1 - dp_index
+    mine = lax.dynamic_index_in_dim(adapter_store, local_slot[dp_index], 0, keepdims=False)
+    theirs = lax.dynamic_index_in_dim(adapter_store, local_slot[other], 0, keepdims=False)
+    swapped = lax.ppermute(theirs, "dp", [(0, 1), (1, 0)])
+    adapter = jnp.where(holder[dp_index] == dp_index, mine, swapped)
+    down = adapter[:, :RANK]
+    up = jnp.transpose(
+        adapter[:, RANK:].reshape(tp_count, local_width, RANK), (0, 2, 1)
+    )
+    row_chip = jnp.repeat(slot_chip[dp_index][request_slot[0]], 2)
+    chip = jnp.broadcast_to(row_chip[:, None], (rows, 128))
+
+    query_width = device_heads * HEAD_WIDTH
+    shared_width = device_heads * KEY_VALUE_SHARE
+    used = query_width + shared_width + RANK
+    columns = -(-used // COLUMN_TILE) * COLUMN_TILE
+    weight = jnp.concatenate(
+        [
+            w_qkv[:, :, :HEAD_WIDTH].reshape(D, query_width),
+            w_qkv[:, :, HEAD_WIDTH:].reshape(D, shared_width),
+            down,
+            jnp.zeros((D, columns - used), jnp.bfloat16),
+        ],
+        axis=1,
+    ).reshape(tp_count, local_width, columns)
+    gain = lax.dynamic_slice_in_dim(norm_gain, column_start, local_width, 0)
+    gain = gain.astype(jnp.float32)[None, :]
+    query, shared = project_rows(
+        tp_count, hidden[0].reshape(rows, local_width), gain, weight, up, chip
+    )
+    query = query.reshape(tp_count, local_requests, 2, device_heads, HEAD_WIDTH)
+    query = jnp.transpose(query, (1, 2, 0, 3, 4)).reshape(local_requests, 2 * HEADS, HEAD_WIDTH)
+    shared = jnp.transpose(
+        shared.reshape(tp_count, local_requests, 2, shared_width), (1, 2, 0, 3)
+    ).reshape(local_requests, 2, HEADS * KEY_VALUE_SHARE)
+    half = KV_HEADS * HEAD_WIDTH
+    lengths = cache_len[0]
+    positions = (lengths[:, None] + jnp.arange(2, dtype=jnp.int32)[None, :]).astype(jnp.float32)
+    counter = jnp.arange(HEAD_WIDTH // 2, dtype=jnp.float32)
+    inverse_freq = rope_base ** (-2.0 * counter / HEAD_WIDTH)
+    angles = positions[..., None] * inverse_freq
+    cosine, sine = jnp.cos(angles), jnp.sin(angles)
+    cos_wide = jnp.concatenate([cosine, cosine], axis=-1)
+    sin_wide = jnp.concatenate([-sine, sine], axis=-1)
+    key_new = shared[..., :half].reshape(local_requests, 2, KV_HEADS, HEAD_WIDTH)
+    key_wide = key_new.astype(jnp.float32)
+    key_turned = jnp.roll(key_wide, HEAD_WIDTH // 2, axis=-1)
+    key_rot = (
+        key_wide * cos_wide[:, :, None, :] + key_turned * sin_wide[:, :, None, :]
+    ).astype(jnp.bfloat16)
+    new_kv = jnp.concatenate(
+        [key_rot.reshape(local_requests, 2, half), shared[..., half:]], axis=-1
+    )
+    new_padded = jnp.pad(new_kv, ((0, 0), (0, 14), (0, 0)))
+    attended = attend_rows(lengths, query, cos_wide, sin_wide, new_padded, cache_kv[0])
+    attn_out = attended.reshape(local_requests, 2, HEADS * HEAD_WIDTH)
+    return (attn_out[None], new_kv[None])
+
+
+def body(tp_count, dp_count, hidden, norm_gain, w_qkv, *rest):
+    rows = hidden.shape[1] * 2
+    shared_width = w_qkv.shape[1] * KEY_VALUE_SHARE
+    fits = (
+        dp_count == 2
+        and tp_count % 2 == 0
+        and rows % (tp_count * 16) == 0
+        and rows % 128 == 0
+        and rows <= 1024
+        and hidden.shape[3] % 128 == 0
+        and shared_width % 128 == 0
+        and (rows // 2) % (SPLIT * 16) == 0
+    )
+    if fits:
+        return ring_body(tp_count, dp_count, hidden, norm_gain, w_qkv, *rest)
+    return plain_body(hidden, norm_gain, w_qkv, *rest)
+
+
 def solution(mesh):
     placed = (
         P(("group", "dp"), None, None, "tp"),
@@ -186,7 +729,7 @@
         P(("group", "dp"), "tp"),
     )
     return jax.shard_map(
-        body,
+        functools.partial(body, mesh.shape["tp"], mesh.shape["dp"]),
         mesh=mesh,
         in_specs=placed,
         out_specs=(P(("group", "dp"), "tp", None, None), P(("group", "dp"), "tp", None, None)),

time: 484 us -> 395 us (0.82)
  the two profiles are of different devices: /device:TPU:0 before, /device:TPU:14 now
where the time goes in v1:
time: 395 us; the launch traced here: 393 us
  Pallas kernels  241 us (61%)
  local copies, waits for them, and re-layouts  134 us (34%)
  other arithmetic  12.1 us (3%)
  between operations  5.38 us (1%)
    pallas_call x1, Pallas kernels, project_rows(): pl.pallas_call(functools.partial(project_kernel, n), out_shape=(jax.Shape...  210 us
    concatenate x3, local copies, waits for them, and re-layouts, ring_body(): jnp.concatenate([w_qkv[:, :, :HEAD_WIDTH].reshape(D, query_width), w_qkv[...  65.9 us
    pallas_call x1, Pallas kernels, attend_rows(): pl.pallas_call(attend_kernel, grid=(requests // block,), out_shape=jax.Sh...  30.9 us
    unnamed x13, local copies, waits for them, and re-layouts  28.2 us
    slice x1, local copies, waits for them, and re-layouts, ring_body(): w_qkv[:, :, :HEAD_WIDTH].reshape(D, query_width)  13.9 us
  transfers between devices with their start and end apart: 1, of which 0 were waited for; matrix products, arithmetic and copies ran while one was open for 23% of the time, Pallas kernels for 0%

profile of v1, /device:TPU:14, one launch (start us, length us, event | category | flops | bytes accessed | tf_op | source)
XLA Modules:
  0.0 392.7 jit_solution(4389058944061871186)
XLA Ops:
  0.7 0.7 compare_select_fusion.7
  1.3 0.1 reshape.106
  1.4 0.7 gather_fusion
  2.1 0.1 reshape.149
  2.3 0.1 reshape.169
  2.4 0.1 fusion.1
  2.5 0.6 fusion.6
  5.0 1.7 dynamic-slice_bitcast_fusion
  8.2 13.9 %slice.26 = bf16[8192,8,128]{0,2,1:T(8,128)(2,1)} slice(bf16[8192,8,160]{0,2,1:T(8,128)(2,1)} %param.11), slice={[0:8192], [0:8], [0:128]} | slice | bytes 33554432 | tf_op jit(solution)/shard_map/slice | solution.py:660
  22.0 4.7 %slice.27 = bf16[8192,8,32]{0,2,1:T(8,128)(2,1)} slice(bf16[8192,8,160]{0,2,1:T(8,128)(2,1)} %param.11), slice={[0:8192], [0:8], [128:160]} | slice | bytes 8388608 | tf_op jit(solution)/shard_map/slice | solution.py:661
  26.7 0.6 dynamic_slice.23
  27.9 18.6 %copy.31 = bf16[128,8,8,1024]{3,2,1,0:T(8,128)(2,1)} copy(bf16[128,8,8,1024]{3,1,2,0:T(8,128)(2,1)} %bitcast.58) | data formatting | bytes 33554432
  46.6 23.2 %copy.27 = bf16[8,1024,1024]{2,1,0:T(8,128)(2,1)} copy(bf16[8,1024,1024]{1,0,2:T(8,128)(2,1)} %bitcast.59) | data formatting | bytes 33554432 | tf_op jit(solution)/shard_map/concatenate | solution.py:658
  69.8 8.5 %copy.32 = bf16[32,8,8,1024]{3,2,1,0:T(8,128)(2,1)} copy(bf16[32,8,8,1024]{3,1,2,0:T(8,128)(2,1)} %bitcast.61) | data formatting | bytes 8388608
  78.3 6.9 %copy.22 = bf16[8,1024,256]{2,1,0:T(8,128)(2,1)} copy(bf16[8,1024,256]{1,0,2:T(8,128)(2,1)} %bitcast.62) | data formatting | bytes 8388608 | tf_op jit(solution)/shard_map/concatenate | solution.py:658
  85.2 0.7 fusion.5
  85.9 4.3 %fusion = s32[384]{0:T(512)S(1)} fusion(s32[]{:T(128)} %bitcast.12, s32[]{:T(128)} %bitcast.13, s32[]{:T(128)} %bitcast.14, s32[]{:T(128)} %bitcast.15, s32[]{:T(128)} %bitcast.16, s32[]{:T(128)} %bitcast.18, s32[]{:T(128)} %bitcast.17, s32[1,384]{1,0:T(1,128)S(1)} %copy-done.4), kind=kLoop, calls=%fused_computation.28 | loop fusion | flops 5760 | bytes 3100 | tf_op jit(solution)/shard_map/gather | solution.py:651
  90.2 0.7 broadcast_select_fusion
  90.9 0.1 broadcast_in_dim.36
  91.0 0.1 broadcast_in_dim.37
  91.1 3.6 reshape_squeeze.3.hidden_ref
  94.9 0.8 fusion.2
  95.7 0.2 pad_maximum_fusion.1
  95.9 0.2 mul.47
  96.7 1.3 dynamic-slice_convert_fusion
  98.0 1.8 bitcast_select_fusion
  99.8 2.1 fusion.3
  101.9 2.7 copy.24
  104.6 2.2 broadcast_in_dim.35
  106.8 35.9 %concatenate.26.weight_ref = bf16[8,1024,1536]{2,1,0:T(8,128)(2,1)} concatenate(bf16[8,1024,1024]{2,1,0:T(8,128)(2,1)} %copy.27, bf16[8,1024,256]{2,1,0:T(8,128)(2,1)} %copy.22, bf16[8,1024,64]{2,1,0:T(8,128)(2,1)S(1)} %bitcast.63, bf16[8,1024,192]{2,1,0:T(8,128)(2,1)} %broadcast_in_dim.35), dimensions={2} | concatenate | bytes 50331648 | tf_op jit(solution)/shard_map/concatenate | solution.py:658
  142.7 0.9 broadcast_in_dim.38.chip_ref
  143.6 210.2 %shard_map.104 = (bf16[8,96,1024]{2,1,0:T(8,128)(2,1)}, bf16[8,96,256]{2,1,0:T(8,128)(2,1)}) custom-call(bf16[768,1024]{1,0:T(8,128)(2,1)} %reshape_squeeze.3.hidden_ref, f32[1,1024]{1,0:T(1,128)} %bitcast.69, bf16[8,1024,1536]{2,1,0:T(8,128)(2,1)} %concatenate.26.weight_ref, bf16[8,64,1024]{2,1,0:T(8,128)(2,1)} %bitcast.68, ...), custom_call_target="tpu_custom_call" | custom-call | flops 19327352832 | bytes 25165824 | tf_op jit(solution)/shard_map/pallas_call | solution.py:485
  353.8 1.2 copy.30
  355.0 0.1 reshape.101
  355.1 0.3 slice_convert_fusion
  355.4 0.3 reshape.103
  355.7 0.2 fusion.4
  355.9 0.2 maximum_multiply_fusion
  356.1 0.2 mul.51
  356.3 0.3 add_convert_fusion
  356.6 1.1 fusion.7
  357.7 0.3 pad_maximum_fusion
  358.0 0.5 pad.4.new_ref
  358.5 0.5 copy-done.3
  359.1 0.4 copy.33
  359.5 0.5 copy.25
  360.0 30.9 %shard_map.105 = bf16[48,128,128]{2,1,0:T(8,128)(2,1)S(1)} custom-call(s32[48]{0:T(128)S(1)} %bitcast.57, bf16[48,128,128]{2,1,0:T(8,128)(2,1)S(1)} %bitcast.55, f32[48,2,128]{2,1,0:T(2,128)S(1)} %get-tuple-element.31.cos_ref, f32[48,2,128]{2,1,0:T(2,128)S(1)} %get-tuple-element.32.sin_ref, bf16[48,16,2048]{2,1,0:T(8,128)(2,1)S(1)} %pad.4.new_ref, ...), custom_call_target="tpu_custom_call" | custom-call | flops 3221225472 | bytes 25165824 | tf_op jit(solution)/shard_map/pallas_call | solution.py:593
  390.9 1.8 broadcast_in_dim_reshape.4
  (21 shorter events, 0.4 us)
Async XLA Ops:
  0.6 0.8 copy-start
  6.8 91.2 %collective-permute-start = (bf16[8192,128]{1,0:T(8,128)(2,1)S(1)}, bf16[8192,128]{1,0:T(8,128)(2,1)}, u32[]{:S(2)}, u32[]{:S(2)}) collective-permute-start(bf16[8192,128]{1,0:T(8,128)(2,1)S(1)} %dynamic-slice_bitcast_fusion), channel_id=1, source_target_pairs={{0,1},{1,0},{2,3},{3,2},{4,5},{5,4},{6,7},{7,6},{8,9},{9,8},{10,11... | collective-permute-start | bytes 6291464 | tf_op jit(solution)/shard_map/ppermute | solution.py:645
  78.3 7.5 %copy-start.4 = (s32[1,384]{1,0:T(1,128)S(1)}, s32[1,384]{1,0:T(1,128)}, u32[]{:S(2)}) copy-start(s32[1,384]{1,0:T(1,128)} %param.15) | copy-start | bytes 4612
  85.2 9.6 %copy-start.2 = (s32[1,48]{1,0:T(1,128)S(1)}, s32[1,48]{1,0:T(1,128)}, u32[]{:S(2)}) copy-start(s32[1,48]{1,0:T(1,128)} %param.17) | copy-start | bytes 580
  357.7 1.4 copy-start.3
  360.0 32.7 %copy-start.1 = (s32[48]{0:T(128)S(1)}, s32[48]{0:T(128)}, u32[]{:S(2)}) copy-start(s32[48]{0:T(128)} %param.13) | copy-start | bytes 580

commit v2 on v1

--- a/solution.py
+++ b/solution.py
@@ -192,7 +192,7 @@
     hidden_ref,
     gain_ref,
     weight_ref,
-    up_ref,
+    adapter_ref,
     chip_ref,
     query_out,
     shared_out,
@@ -253,13 +253,30 @@
     for d in range(1, n):
         pl.semaphore_signal(barrier, inc=1, device_id={"tp": peer(d)}, device_id_type=MESH_ID)
 
-    def weight_copy(block):
-        return pltpu.make_async_copy(
-            weight_ref.at[block], weight_buf.at[block], weight_sem.at[block]
-        )
-
-    for block in range(n):
-        weight_copy(block).start()
+    heads = weight_ref.shape[0]
+    low_column = query_width + shared_width
+    adapter_copy = pltpu.make_async_copy(
+        adapter_ref, weight_buf.at[pl.ds(low_column, 2 * RANK)], weight_sem.at[2 * heads]
+    )
+    adapter_copy.start()
+
+    def weight_copies(head):
+        return (
+            pltpu.make_async_copy(
+                weight_ref.at[head, pl.ds(0, HEAD_WIDTH)],
+                weight_buf.at[pl.ds(head * HEAD_WIDTH, HEAD_WIDTH)],
+                weight_sem.at[2 * head],
+            ),
+            pltpu.make_async_copy(
+                weight_ref.at[head, pl.ds(HEAD_WIDTH, KEY_VALUE_SHARE)],
+                weight_buf.at[pl.ds(query_width + head * KEY_VALUE_SHARE, KEY_VALUE_SHARE)],
+                weight_sem.at[2 * head + 1],
+            ),
+        )
+
+    for head in range(heads):
+        for copy in weight_copies(head):
+            copy.start()
 
     sums_send[...] = jnp.zeros_like(sums_send)
     for i in range(rows // 128):
@@ -318,31 +335,43 @@
     def compute(i):
         parts = [ring_part(direction, i) for direction in range(2)]
 
-        @pl.loop(0, total.shape[1] // COLUMN_TILE)
-        def _(j):
-            columns = pl.ds(pl.multiple_of(j * COLUMN_TILE, COLUMN_TILE), COLUMN_TILE)
+        def add(columns):
             for owner, span in parts:
-                total[span, columns] += jnp.dot(
+                features = pl.ds(pl.multiple_of(owner * width, width), width)
+                total[span, columns] += lax.dot_general(
                     normed[owner, span, :],
-                    weight_buf[owner, :, columns],
+                    weight_buf[columns, features],
+                    (((1,), (1,)), ((), ())),
                     preferred_element_type=jnp.float32,
                 )
+
+        @pl.loop(0, low_column // COLUMN_TILE)
+        def _(j):
+            add(pl.ds(pl.multiple_of(j * COLUMN_TILE, COLUMN_TILE), COLUMN_TILE))
+
+        add(pl.ds(low_column, 2 * RANK))
 
     for i in range(SPLIT):
         for direction in range(2):
             ring_copy(direction, i).start()
 
+    def up_slice(t):
+        features = pl.ds(pl.multiple_of(t * width, width), width)
+        return weight_buf.at[pl.ds(low_column + RANK, RANK), features]
+
     def up_copy(d):
         return remote(
-            up_ref.at[peer(d)], up_all.at[me], up_send_sem.at[d], up_recv_sem.at[d], peer(d)
-        )
-
+            up_slice(peer(d)), up_all.at[me], up_send_sem.at[d], up_recv_sem.at[d], peer(d)
+        )
+
+    adapter_copy.wait()
     for d in range(1, n):
         up_copy(d).start()
-    up_all[me] = up_ref[me]
+    up_all[me] = up_slice(me)[...]
     total[...] = jnp.zeros_like(total)
-    for block in range(n):
-        weight_copy(block).wait()
+    for head in range(heads):
+        for copy in weight_copies(head):
+            copy.wait()
 
     def first(i, _):
         compute(i)
@@ -367,11 +396,13 @@
 
     lax.fori_loop((n - 1) * SPLIT, n * SPLIT, last, 0)
 
-    low_column = query_width + shared_width
+    lane = lax.broadcasted_iota(jnp.int32, (own_rows, 128), 1)
     for t in range(n):
         span = slice(t * own_rows, (t + 1) * own_rows)
         low = total[span, low_column : low_column + 128]
-        reduce_send[span, :] = jnp.where(chip_ref[span, :] == me, low, 0.0).astype(jnp.bfloat16)
+        reduce_send[span, :] = jnp.where(
+            (chip_ref[span, :] == me) & (lane < RANK), low, 0.0
+        ).astype(jnp.bfloat16)
 
     def reduce_copy(d):
         return remote(
@@ -473,14 +504,16 @@
         query_copy(d).wait_send()
 
 
-def project_rows(n, hidden, gain, weight, up, chip):
+def project_rows(n, hidden, gain, weight, adapter, chip):
     rows, width = hidden.shape
-    columns = weight.shape[2]
+    heads = weight.shape[0]
     own_rows = rows // n
-    query_width = up.shape[2]
-    shared_width = query_width // HEAD_WIDTH * KEY_VALUE_SHARE
+    query_width = heads * HEAD_WIDTH
+    shared_width = heads * KEY_VALUE_SHARE
+    columns = query_width + shared_width + 2 * RANK
     dma = pltpu.SemaphoreType.DMA
     vmem = pl.BlockSpec(memory_space=pltpu.VMEM)
+    hbm = pl.BlockSpec(memory_space=pl.ANY)
     bf16, f32 = jnp.bfloat16, jnp.float32
     return pl.pallas_call(
         functools.partial(project_kernel, n),
@@ -488,11 +521,11 @@
             jax.ShapeDtypeStruct((n, own_rows, query_width), bf16),
             jax.ShapeDtypeStruct((n, own_rows, shared_width), bf16),
         ),
-        in_specs=[vmem, vmem, pl.BlockSpec(memory_space=pl.ANY), vmem, vmem],
+        in_specs=[vmem, vmem, hbm, hbm, vmem],
         out_specs=(vmem, vmem),
         scratch_shapes=[
             pltpu.VMEM((n, rows, width), bf16),
-            pltpu.VMEM((n, width, columns), bf16),
+            pltpu.VMEM((columns, n * width), bf16),
             pltpu.VMEM((rows, columns), f32),
             pltpu.VMEM((rows, query_width), bf16),
             pltpu.VMEM((rows, shared_width), bf16),
@@ -502,7 +535,7 @@
             pltpu.VMEM((rows, 128), bf16),
             pltpu.VMEM((n, own_rows, 128), bf16),
             pltpu.VMEM((n, own_rows, 128), bf16),
-            dma((n,)),
+            dma((2 * heads + 1,)),
             dma((2, (n - 1) * SPLIT)),
             dma((2, (n - 1) * SPLIT)),
         ]
@@ -515,7 +548,7 @@
             bytes_accessed=2 * n * width * columns,
             transcendentals=0,
         ),
-    )(hidden, gain, weight, up, chip)
+    )(hidden, gain, weight, adapter, chip)
 
 
 def attend_kernel(
@@ -644,30 +677,20 @@
     theirs = lax.dynamic_index_in_dim(adapter_store, local_slot[other], 0, keepdims=False)
     swapped = lax.ppermute(theirs, "dp", [(0, 1), (1, 0)])
     adapter = jnp.where(holder[dp_index] == dp_index, mine, swapped)
-    down = adapter[:, :RANK]
-    up = jnp.transpose(
-        adapter[:, RANK:].reshape(tp_count, local_width, RANK), (0, 2, 1)
-    )
-    row_chip = jnp.repeat(slot_chip[dp_index][request_slot[0]], 2)
+    slots = jnp.arange(slot_adapter.shape[1], dtype=jnp.int32)
+    block_chip = lax.dynamic_index_in_dim(slot_chip, dp_index, 0, keepdims=False)
+    request_chip = jnp.sum(
+        jnp.where(request_slot[0][:, None] == slots, block_chip, 0), axis=1, dtype=jnp.int32
+    )
+    row_chip = jnp.repeat(request_chip, 2)
     chip = jnp.broadcast_to(row_chip[:, None], (rows, 128))
 
-    query_width = device_heads * HEAD_WIDTH
     shared_width = device_heads * KEY_VALUE_SHARE
-    used = query_width + shared_width + RANK
-    columns = -(-used // COLUMN_TILE) * COLUMN_TILE
-    weight = jnp.concatenate(
-        [
-            w_qkv[:, :, :HEAD_WIDTH].reshape(D, query_width),
-            w_qkv[:, :, HEAD_WIDTH:].reshape(D, shared_width),
-            down,
-            jnp.zeros((D, columns - used), jnp.bfloat16),
-        ],
-        axis=1,
-    ).reshape(tp_count, local_width, columns)
+    weight = jnp.transpose(w_qkv, (1, 2, 0))
     gain = lax.dynamic_slice_in_dim(norm_gain, column_start, local_width, 0)
     gain = gain.astype(jnp.float32)[None, :]
     query, shared = project_rows(
-        tp_count, hidden[0].reshape(rows, local_width), gain, weight, up, chip
+        tp_count, hidden[0].reshape(rows, local_width), gain, weight, adapter.T, chip
     )
     query = query.reshape(tp_count, local_requests, 2, device_heads, HEAD_WIDTH)
     query = jnp.transpose(query, (1, 2, 0, 3, 4)).reshape(local_requests, 2 * HEADS, HEAD_WIDTH)

time: 395 us -> 278 us (0.70)
  local copies, waits for them, and re-layouts: 134 us -> 22.2 us
  other arithmetic: 12.1 us -> 6.97 us
    concatenate x3 -> x0, local copies, waits for them, and re-layouts: 65.9 us -> none  [ring_body(): jnp.concatenate([w_qkv[:, :, :HEAD_WIDTH].reshape(D, query_width), w_qkv[...]
    unnamed x13 -> x11, local copies, waits for them, and re-layouts: 28.2 us -> 0.47 us
    slice x3 -> x0, local copies, waits for them, and re-layouts: 20.6 us -> none  [the longest x1 13.9 us: ring_body(): w_qkv[:, :, :HEAD_WIDTH].reshape(D, query_width)]
    dynamic_slice x1 -> x3, local copies, waits for them, and re-layouts: 0.01 us -> 9.65 us  [the longest x2 6.74 us: ring_body(): lax.dynamic_index_in_dim(adapter_store, local_slot[dp_index], 0, keepdims...]
    gather x3 -> x0, other arithmetic: 5 us -> none  [ring_body(): row_chip = jnp.repeat(slot_chip[dp_index][request_slot[0]], 2)]
  transfers between devices with their start and end apart: 1 -> 1, of which waited for: 0 -> 0; matrix products, arithmetic and copies ran while one was open for 23% -> 4% of each run, Pallas kernels for 0% -> 0%
where the time goes in v2:
time: 278 us; the launch traced here: 277 us
  Pallas kernels  243 us (87%)
  local copies, waits for them, and re-layouts  22.2 us (8%)
  other arithmetic  6.97 us (3%)
  between operations  5.4 us (2%)
    pallas_call x1, Pallas kernels, project_rows(): pl.pallas_call(functools.partial(project_kernel, n), out_shape=(jax.Shape...  212 us
    pallas_call x1, Pallas kernels, attend_rows(): pl.pallas_call(attend_kernel, grid=(requests // block,), out_shape=jax.Sh...  30.9 us
    dynamic_slice x2, local copies, waits for them, and re-layouts, ring_body(): lax.dynamic_index_in_dim(adapter_store, local_slot[dp_index], 0, keepdims...  6.74 us
  transfers between devices with their start and end apart: 1, of which 0 were waited for; matrix products, arithmetic and copies ran while one was open for 4% of the time, Pallas kernels for 0%

profile of v2, /device:TPU:14, one launch (start us, length us, event | category | flops | bytes accessed | tf_op | source)
XLA Modules:
  0.0 277.4 jit_solution(1169125359437513829)
XLA Ops:
  0.6 0.0 copy-start
  0.7 0.7 compare_select_fusion
  1.3 0.1 reshape.66
  1.4 0.0 copy-done
  1.4 0.7 gather_fusion
  2.1 0.1 reshape.76
  2.2 0.1 reshape.78
  2.3 0.1 reshape.80
  2.4 0.1 fusion.1
  2.5 0.6 fusion.5
  7.0 3.8 %constant_dynamic-slice_fusion.2 = (bf16[1,8192,128]{2,1,0:T(8,128)(2,1)}, bf16[1,8192,128]{2,1,0:T(8,128)(2,1)S(1)}) fusion(bf16[3,8192,128]{2,1,0:T(8,128)(2,1)} %param.12, s32[]{:T(128)S(6)} %select_n.70, s32[]{:T(128)S(6)} %select_n.72), kind=kLoop, calls=%fused_computation.25 | loop fusion | bytes 8388616 | tf_op jit(solution)/shard_map/jit(dynamic_index_in_dim)/dynamic_slice | solution.py:676
  10.8 2.9 %copy.20 = bf16[1,8192,128]{1,2,0:T(8,128)(2,1)} copy(bf16[1,8192,128]{2,1,0:T(8,128)(2,1)S(1)} %get-tuple-element.9) | data formatting | bytes 4194304 | tf_op jit(solution)/shard_map/jit(dynamic_index_in_dim)/dynamic_slice | solution.py:677
  13.7 0.0 collective-permute-start
  13.7 2.9 %copy.19 = bf16[1,8192,128]{1,2,0:T(8,128)(2,1)S(1)} copy(bf16[1,8192,128]{2,1,0:T(8,128)(2,1)} %get-tuple-element.8) | data formatting | bytes 4194304 | tf_op jit(solution)/shard_map/jit(dynamic_index_in_dim)/dynamic_slice | solution.py:676
  16.6 0.0 copy-start.2
  16.7 0.6 dynamic_slice.24
  17.9 0.0 copy-done.4
  17.9 0.1 select_reduce_fusion
  18.0 0.1 broadcast_in_dim.42
  18.1 0.1 broadcast_in_dim.43
  18.3 3.6 %reshape_squeeze.3.hidden_ref = bf16[768,1024]{1,0:T(8,128)(2,1)} reshape(bf16[1,384,2,1024]{3,2,1,0:T(2,128)(2,1)} %param.9) | data formatting | bytes 3145728 | tf_op jit(solution)/shard_map/reshape;squeeze | solution.py:693
  22.0 0.0 copy-done.2
  22.0 0.1 add_convert_fusion.1
  22.0 0.8 fusion.3
  22.8 0.2 pad_maximum_fusion.1
  23.0 0.2 mul.47
  23.2 1.3 dynamic-slice_convert_fusion
  24.5 0.0 collective-permute-done
  24.5 1.6 fusion.adapter_ref
  26.1 0.9 broadcast_in_dim.44.chip_ref
  27.0 212.0 %shard_map.104 = (bf16[8,96,1024]{2,1,0:T(8,128)(2,1)}, bf16[8,96,256]{2,1,0:T(8,128)(2,1)}) custom-call(bf16[768,1024]{1,0:T(8,128)(2,1)} %reshape_squeeze.3.hidden_ref, f32[1,1024]{1,0:T(1,128)} %bitcast.42, bf16[8,160,8192]{2,1,0:T(8,128)(2,1)} %bitcast.43, bf16[128,8192]{1,0:T(8,128)(2,1)} %fusion.adapter_ref, s32[768,128]{1,0:T(8,128)} %broadcast_in_dim.44.chip_ref), custom_call_target="tpu_custom_call" | custom-call | flops 17716740096 | bytes 23068672 | tf_op jit(solution)/shard_map/pallas_call | solution.py:518
  239.0 1.2 copy.23
  240.2 0.1 reshape.61
  240.3 0.3 slice_convert_fusion
  240.6 0.3 reshape.63
  240.9 0.2 fusion.4
  241.1 0.0 copy-start.3
  241.1 0.2 maximum_multiply_fusion
  241.3 0.2 mul.51
  241.5 0.3 add_convert_fusion
  241.8 1.1 fusion.6
  242.9 0.3 pad_maximum_fusion
  243.2 0.4 copy.24
  243.7 0.5 copy.21
  244.1 0.5 pad.4.new_ref
  244.6 0.0 copy-start.1
  244.7 30.9 %shard_map.105 = bf16[48,128,128]{2,1,0:T(8,128)(2,1)S(1)} custom-call(s32[48]{0:T(128)S(1)} %bitcast.36, bf16[48,128,128]{2,1,0:T(8,128)(2,1)S(1)} %bitcast.34, f32[48,2,128]{2,1,0:T(2,128)S(1)} %get-tuple-element.23.cos_ref, f32[48,2,128]{2,1,0:T(2,128)S(1)} %get-tuple-element.24.sin_ref, bf16[48,16,2048]{2,1,0:T(8,128)(2,1)S(1)} %pad.4.new_ref, ...), custom_call_target="tpu_custom_call" | custom-call | flops 3221225472 | bytes 25165824 | tf_op jit(solution)/shard_map/pallas_call | solution.py:626
  275.5 1.8 broadcast_in_dim_reshape.4
  (11 shorter events, 0.1 us)
Async XLA Ops:
  0.6 0.8 copy-start
  13.7 10.8 %collective-permute-start = (bf16[8192,128]{0,1:T(8,128)(2,1)}, bf16[8192,128]{0,1:T(8,128)(2,1)}, u32[]{:S(2)}, u32[]{:S(2)}) collective-permute-start(bf16[8192,128]{0,1:T(8,128)(2,1)} %bitcast.39), channel_id=1, source_target_pairs={{0,1},{1,0},{2,3},{3,2},{4,5},{5,4},{6,7},{7,6},{8,9},{9,8},{10,11... | collective-permute-start | bytes 6291464 | tf_op jit(solution)/shard_map/ppermute | solution.py:678
  13.7 4.2 %copy-start.4 = (s32[1,384]{1,0:T(1,128)S(1)}, s32[1,384]{1,0:T(1,128)}, u32[]{:S(2)}) copy-start(s32[1,384]{1,0:T(1,128)} %param.15) | copy-start | bytes 4612
  16.6 5.3 %copy-start.2 = (s32[1,48]{1,0:T(1,128)S(1)}, s32[1,48]{1,0:T(1,128)}, u32[]{:S(2)}) copy-start(s32[1,48]{1,0:T(1,128)} %param.17) | copy-start | bytes 580
  241.1 2.1 copy-start.3
  244.6 32.7 %copy-start.1 = (s32[48]{0:T(128)S(1)}, s32[48]{0:T(128)}, u32[]{:S(2)}) copy-start(s32[48]{0:T(128)} %param.13) | copy-start | bytes 580

commit v3 on v2

--- a/solution.py
+++ b/solution.py
@@ -291,8 +291,21 @@
             sums_send, sums_all.at[me], sums_send_sem.at[d], sums_recv_sem.at[d], peer(d)
         )
 
+    def up_slice(t):
+        features = pl.ds(pl.multiple_of(t * width, width), width)
+        return weight_buf.at[pl.ds(low_column + RANK, RANK), features]
+
+    def up_copy(d):
+        return remote(
+            up_slice(peer(d)), up_all.at[me], up_send_sem.at[d], up_recv_sem.at[d], peer(d)
+        )
+
     for d in range(1, n):
         sums_copy(d).start()
+    adapter_copy.wait()
+    for d in range(1, n):
+        up_copy(d).start()
+    up_all[me] = up_slice(me)[...]
     for d in range(1, n):
         sums_copy(d).wait_recv()
     sums = sums_all[0]
@@ -355,19 +368,6 @@
         for direction in range(2):
             ring_copy(direction, i).start()
 
-    def up_slice(t):
-        features = pl.ds(pl.multiple_of(t * width, width), width)
-        return weight_buf.at[pl.ds(low_column + RANK, RANK), features]
-
-    def up_copy(d):
-        return remote(
-            up_slice(peer(d)), up_all.at[me], up_send_sem.at[d], up_recv_sem.at[d], peer(d)
-        )
-
-    adapter_copy.wait()
-    for d in range(1, n):
-        up_copy(d).start()
-    up_all[me] = up_slice(me)[...]
     total[...] = jnp.zeros_like(total)
     for head in range(heads):
         for copy in weight_copies(head):
@@ -551,46 +551,53 @@
     )(hidden, gain, weight, adapter, chip)
 
 
-def attend_kernel(
-    length_ref, query_ref, cos_ref, sin_ref, new_ref, cache_ref, out_ref
-):
+CACHE_PARTS = 4
+
+
+def attend_kernel(length_ref, query_ref, cos_ref, sin_ref, new_ref, *rest):
+    cache_refs, out_ref = rest[:CACHE_PARTS], rest[CACHE_PARTS]
     count = query_ref.shape[0]
     lanes = KV_HEADS * HEAD_WIDTH
+    part_width = 2 * lanes // CACHE_PARTS
     pad = new_ref.shape[1]
     first = pl.program_id(0) * count
     factor = HEAD_WIDTH ** (-0.5)
-    row = lax.broadcasted_iota(jnp.int32, (2 * HEADS, lanes), 0)
-    lane = lax.broadcasted_iota(jnp.int32, (2 * HEADS, lanes), 1)
-    own = (row // GROUP) % KV_HEADS == lane // HEAD_WIDTH
+    group_rows = 2 * GROUP
     key_at = lax.broadcasted_iota(jnp.int32, (2 * HEADS, CACHE), 1)
     new_at = lax.broadcasted_iota(jnp.int32, (2 * HEADS, pad), 1)
-    new_limit = lax.broadcasted_iota(jnp.int32, (2 * HEADS, pad), 0) // HEADS
+    new_limit = (lax.broadcasted_iota(jnp.int32, (2 * HEADS, pad), 0) // GROUP) % 2
+    second = (lax.broadcasted_iota(jnp.int32, (2 * HEADS, HEAD_WIDTH), 0) // GROUP) % 2 == 1
     across = (((1,), (1,)), ((), ()))
+
+    def cached(b, start):
+        within = start % part_width
+        return cache_refs[start // part_width][b, :, within : within + HEAD_WIDTH]
+
     for b in range(count):
         query = query_ref[b].astype(jnp.float32)
         turned = pltpu.roll(query, HEAD_WIDTH // 2, 1)
-        rotated = jnp.concatenate(
-            [
-                query[p * HEADS : (p + 1) * HEADS] * cos_ref[b, p : p + 1, :]
-                + turned[p * HEADS : (p + 1) * HEADS] * sin_ref[b, p : p + 1, :]
-                for p in range(2)
-            ],
-            axis=0,
-        ).astype(jnp.bfloat16)
-        wide = jnp.concatenate([rotated] * KV_HEADS, axis=1)
-        wide = jnp.where(own, wide, jnp.zeros((), jnp.bfloat16))
-        old = (
-            lax.dot_general(
-                wide, cache_ref[b, :, 0:lanes], across, preferred_element_type=jnp.float32
+        cosine = jnp.where(second, cos_ref[b, 1:2, :], cos_ref[b, 0:1, :])
+        sine = jnp.where(second, sin_ref[b, 1:2, :], sin_ref[b, 0:1, :])
+        rotated = (query * cosine + turned * sine).astype(jnp.bfloat16)
+        old, new = [], []
+        for g in range(KV_HEADS):
+            own = rotated[g * group_rows : (g + 1) * group_rows]
+            start = g * HEAD_WIDTH
+            old.append(
+                lax.dot_general(
+                    own, cached(b, start), across, preferred_element_type=jnp.float32
+                )
             )
-            * factor
-        )
-        new = (
-            lax.dot_general(
-                wide, new_ref[b, :, 0:lanes], across, preferred_element_type=jnp.float32
+            new.append(
+                lax.dot_general(
+                    own,
+                    new_ref[b, :, start : start + HEAD_WIDTH],
+                    across,
+                    preferred_element_type=jnp.float32,
+                )
             )
-            * factor
-        )
+        old = jnp.concatenate(old, axis=0) * factor
+        new = jnp.concatenate(new, axis=0) * factor
         old = jnp.where(key_at < length_ref[first + b], old, masked_out)
         new = jnp.where(new_at <= new_limit, new, masked_out)
         highest = jnp.maximum(
@@ -603,25 +610,29 @@
         )
         old_weights = (old_exp / denominator).astype(jnp.bfloat16)
         new_weights = (new_exp / denominator).astype(jnp.bfloat16)
-        mixture = jnp.dot(
-            old_weights, cache_ref[b, :, lanes:], preferred_element_type=jnp.float32
-        ) + jnp.dot(new_weights, new_ref[b, :, lanes:], preferred_element_type=jnp.float32)
-        pieces = []
-        for p in range(2):
-            for g in range(KV_HEADS):
-                start = p * HEADS + g * GROUP
-                pieces.append(
-                    mixture[start : start + GROUP, g * HEAD_WIDTH : (g + 1) * HEAD_WIDTH]
-                )
-        out_ref[b] = jnp.concatenate(pieces, axis=0).astype(jnp.bfloat16)
+        for g in range(KV_HEADS):
+            span = slice(g * group_rows, (g + 1) * group_rows)
+            start = lanes + g * HEAD_WIDTH
+            mixture = jnp.dot(
+                old_weights[span], cached(b, start), preferred_element_type=jnp.float32
+            ) + jnp.dot(
+                new_weights[span],
+                new_ref[b, :, start : start + HEAD_WIDTH],
+                preferred_element_type=jnp.float32,
+            )
+            out_ref[b, span, :] = mixture.astype(jnp.bfloat16)
 
 
 def attend_rows(lengths, query, cosine, sine, new, cache):
     requests = query.shape[0]
-    block = 4
+    block = 8
+    width = cache.shape[2] // CACHE_PARTS
 
     def spec(*shape):
         return pl.BlockSpec((block,) + shape, lambda i: (i,) + (0,) * len(shape))
+
+    def cache_spec(part):
+        return pl.BlockSpec((block, CACHE, width), lambda i: (i, 0, part))
 
     return pl.pallas_call(
         attend_kernel,
@@ -633,16 +644,16 @@
             spec(2, HEAD_WIDTH),
             spec(2, HEAD_WIDTH),
             spec(new.shape[1], new.shape[2]),
-            spec(CACHE, cache.shape[2]),
-        ],
+        ]
+        + [cache_spec(part) for part in range(CACHE_PARTS)],
         out_specs=spec(2 * HEADS, HEAD_WIDTH),
-        compiler_params=pltpu.CompilerParams(vmem_limit_bytes=32 * 1024 * 1024),
+        compiler_params=pltpu.CompilerParams(vmem_limit_bytes=48 * 1024 * 1024),
         cost_estimate=pl.CostEstimate(
-            flops=4 * requests * 2 * HEADS * HEAD_WIDTH * CACHE * KV_HEADS,
+            flops=4 * requests * 2 * HEADS * HEAD_WIDTH * CACHE,
             bytes_accessed=2 * requests * CACHE * cache.shape[2],
             transcendentals=requests * 2 * HEADS * CACHE,
         ),
-    )(lengths, query, cosine, sine, new, cache)
+    )(lengths, query, cosine, sine, new, *([cache] * CACHE_PARTS))
 
 
 def ring_body(
@@ -692,8 +703,12 @@
     query, shared = project_rows(
         tp_count, hidden[0].reshape(rows, local_width), gain, weight, adapter.T, chip
     )
-    query = query.reshape(tp_count, local_requests, 2, device_heads, HEAD_WIDTH)
-    query = jnp.transpose(query, (1, 2, 0, 3, 4)).reshape(local_requests, 2 * HEADS, HEAD_WIDTH)
+    query = query.reshape(
+        tp_count, local_requests, 2, device_heads // GROUP, GROUP, HEAD_WIDTH
+    )
+    query = jnp.transpose(query, (1, 0, 3, 2, 4, 5)).reshape(
+        local_requests, 2 * HEADS, HEAD_WIDTH
+    )
     shared = jnp.transpose(
         shared.reshape(tp_count, local_requests, 2, shared_width), (1, 2, 0, 3)
     ).reshape(local_requests, 2, HEADS * KEY_VALUE_SHARE)
@@ -717,7 +732,10 @@
     )
     new_padded = jnp.pad(new_kv, ((0, 0), (0, 14), (0, 0)))
     attended = attend_rows(lengths, query, cos_wide, sin_wide, new_padded, cache_kv[0])
-    attn_out = attended.reshape(local_requests, 2, HEADS * HEAD_WIDTH)
+    attended = attended.reshape(local_requests, KV_HEADS, 2, GROUP, HEAD_WIDTH)
+    attn_out = jnp.transpose(attended, (0, 2, 1, 3, 4)).reshape(
+        local_requests, 2, HEADS * HEAD_WIDTH
+    )
     return (attn_out[None], new_kv[None])
 
 
@@ -733,6 +751,8 @@
         and hidden.shape[3] % 128 == 0
         and shared_width % 128 == 0
         and (rows // 2) % (SPLIT * 16) == 0
+        and w_qkv.shape[1] % GROUP == 0
+        and rows // (2 * tp_count) % 8 == 0
     )
     if fits:
         return ring_body(tp_count, dp_count, hidden, norm_gain, w_qkv, *rest)

time: 278 us -> 272 us (0.978)
  Pallas kernels: 243 us -> 233 us
  local copies, waits for them, and re-layouts: 22.2 us -> 25.2 us
    pallas_call x1, Pallas kernels: 30.9 us -> 25.7 us  [attend_rows(): pl.pallas_call(attend_kernel, grid=(requests // block,), out_shape=jax.Sh...]
    pallas_call x1, Pallas kernels: 212 us -> 208 us  [project_rows(): pl.pallas_call(functools.partial(project_kernel, n), out_shape=(jax.Shape...]
where the time goes in v3:
time: 272 us
  Pallas kernels  233 us (86%)
  local copies, waits for them, and re-layouts  25.2 us (9%)
  other arithmetic  7.72 us (3%)
  between operations  5.39 us (2%)
    pallas_call x1, Pallas kernels, project_rows(): pl.pallas_call(functools.partial(project_kernel, n), out_shape=(jax.Shape...  208 us
    pallas_call x1, Pallas kernels, attend_rows(): pl.pallas_call(attend_kernel, grid=(requests // block,), out_shape=jax.Sh...  25.7 us
    dynamic_slice x2, local copies, waits for them, and re-layouts, ring_body(): lax.dynamic_index_in_dim(adapter_store, local_slot[dp_index], 0, keepdims...  6.74 us
  transfers between devices with their start and end apart: 1, of which 0 were waited for; matrix products, arithmetic and copies ran while one was open for 4% of the time, Pallas kernels for 0%

profile of v3, /device:TPU:14, one launch (start us, length us, event | category | flops | bytes accessed | tf_op | source)
XLA Modules:
  0.0 271.6 jit_solution(8390136885725327307)
XLA Ops:
  0.6 0.0 copy-start
  0.7 0.7 compare_select_fusion
  1.3 0.1 reshape.70
  1.4 0.0 copy-done
  1.4 0.7 gather_fusion
  2.1 0.1 reshape.80
  2.2 0.1 reshape.82
  2.3 0.1 reshape.84
  2.4 0.1 fusion.1
  2.5 0.6 fusion.5
  7.0 3.8 %constant_dynamic-slice_fusion.2 = (bf16[1,8192,128]{2,1,0:T(8,128)(2,1)}, bf16[1,8192,128]{2,1,0:T(8,128)(2,1)S(1)}) fusion(bf16[3,8192,128]{2,1,0:T(8,128)(2,1)} %param.12, s32[]{:T(128)S(6)} %select_n.70, s32[]{:T(128)S(6)} %select_n.72), kind=kLoop, calls=%fused_computation.25 | loop fusion | bytes 8388616 | tf_op jit(solution)/shard_map/jit(dynamic_index_in_dim)/dynamic_slice | solution.py:687
  10.8 2.9 %copy.22 = bf16[1,8192,128]{1,2,0:T(8,128)(2,1)} copy(bf16[1,8192,128]{2,1,0:T(8,128)(2,1)S(1)} %get-tuple-element.9) | data formatting | bytes 4194304 | tf_op jit(solution)/shard_map/jit(dynamic_index_in_dim)/dynamic_slice | solution.py:688
  13.7 0.0 collective-permute-start
  13.7 2.9 %copy.21 = bf16[1,8192,128]{1,2,0:T(8,128)(2,1)S(1)} copy(bf16[1,8192,128]{2,1,0:T(8,128)(2,1)} %get-tuple-element.8) | data formatting | bytes 4194304 | tf_op jit(solution)/shard_map/jit(dynamic_index_in_dim)/dynamic_slice | solution.py:687
  16.6 0.0 copy-start.2
  16.7 0.6 dynamic_slice.24
  17.9 0.0 copy-done.4
  17.9 0.1 select_reduce_fusion
  18.0 0.1 broadcast_in_dim.42
  18.1 0.1 broadcast_in_dim.43
  18.3 3.6 %reshape_squeeze.3.hidden_ref = bf16[768,1024]{1,0:T(8,128)(2,1)} reshape(bf16[1,384,2,1024]{3,2,1,0:T(2,128)(2,1)} %param.9) | data formatting | bytes 3145728 | tf_op jit(solution)/shard_map/reshape;squeeze | solution.py:704
  22.0 0.0 copy-done.2
  22.0 0.1 add_convert_fusion.1
  22.0 0.8 fusion.3
  22.8 0.2 pad_maximum_fusion.1
  23.0 0.2 mul.47
  23.2 1.3 dynamic-slice_convert_fusion
  24.5 0.0 collective-permute-done
  24.5 1.6 fusion.adapter_ref
  26.1 0.9 broadcast_in_dim.44.chip_ref
  27.0 207.7 %shard_map.104 = (bf16[8,96,1024]{2,1,0:T(8,128)(2,1)}, bf16[8,96,256]{2,1,0:T(8,128)(2,1)}) custom-call(bf16[768,1024]{1,0:T(8,128)(2,1)} %reshape_squeeze.3.hidden_ref, f32[1,1024]{1,0:T(1,128)} %bitcast.52, bf16[8,160,8192]{2,1,0:T(8,128)(2,1)} %bitcast.53, bf16[128,8192]{1,0:T(8,128)(2,1)} %fusion.adapter_ref, s32[768,128]{1,0:T(8,128)} %broadcast_in_dim.44.chip_ref), custom_call_target="tpu_custom_call" | custom-call | flops 17716740096 | bytes 23068672 | tf_op jit(solution)/shard_map/pallas_call | solution.py:518
  234.7 1.2 copy.26
  235.9 0.1 reshape.64
  236.0 0.3 slice_convert_fusion
  236.3 0.3 reshape.67
  236.6 0.2 fusion.4
  236.8 0.9 maximum_multiply_fusion
  237.7 1.2 mul.51
  238.9 0.3 add_convert_fusion
  239.2 1.1 fusion.6
  240.3 0.3 pad_maximum_fusion
  240.7 0.4 copy.27
  241.1 0.5 copy.23
  241.6 2.2 pad.4.new_ref
  243.7 25.7 %shard_map.105 = bf16[48,128,128]{2,1,0:T(8,128)(2,1)S(1)} custom-call(s32[48]{0:T(128)S(1)} %bitcast.43, bf16[48,128,128]{2,1,0:T(8,128)(2,1)S(1)} %bitcast.40, f32[48,2,128]{2,1,0:T(2,128)S(1)} %get-tuple-element.23.cos_ref, f32[48,2,128]{2,1,0:T(2,128)S(1)} %get-tuple-element.24.sin_ref, bf16[48,16,2048]{2,1,0:T(8,128)(2,1)} %pad.4.new_ref, ...), custom_call_target="tpu_custom_call" | custom-call | flops 402653184 | bytes 25165824 | tf_op jit(solution)/shard_map/pallas_call | solution.py:637
  269.4 0.0 copy-start.1
  269.4 0.4 copy.25
  269.8 1.8 broadcast_in_dim_reshape.4
  (12 shorter events, 0.1 us)
Async XLA Ops:
  0.6 0.8 copy-start
  13.7 10.8 %collective-permute-start = (bf16[8192,128]{0,1:T(8,128)(2,1)}, bf16[8192,128]{0,1:T(8,128)(2,1)}, u32[]{:S(2)}, u32[]{:S(2)}) collective-permute-start(bf16[8192,128]{0,1:T(8,128)(2,1)} %bitcast.49), channel_id=1, source_target_pairs={{0,1},{1,0},{2,3},{3,2},{4,5},{5,4},{6,7},{7,6},{8,9},{9,8},{10,11... | collective-permute-start | bytes 6291464 | tf_op jit(solution)/shard_map/ppermute | solution.py:689
  13.7 4.2 %copy-start.4 = (s32[1,384]{1,0:T(1,128)S(1)}, s32[1,384]{1,0:T(1,128)}, u32[]{:S(2)}) copy-start(s32[1,384]{1,0:T(1,128)} %param.15) | copy-start | bytes 4612
  16.6 5.3 %copy-start.2 = (s32[1,48]{1,0:T(1,128)S(1)}, s32[1,48]{1,0:T(1,128)}, u32[]{:S(2)}) copy-start(s32[1,48]{1,0:T(1,128)} %param.17) | copy-start | bytes 580
  236.8 3.9 %copy-start.3 = (bf16[8,96,1024]{2,1,0:T(8,128)(2,1)S(1)}, bf16[8,96,1024]{2,1,0:T(8,128)(2,1)}, u32[]{:S(2)}) copy-start(bf16[8,96,1024]{2,1,0:T(8,128)(2,1)} %get-tuple-element.4) | copy-start | bytes 4718596
  269.4 2.2 copy-start.1
